TPU v7x, 32 devices: a whole 2x2x4 slice. The times are simulated.
32 devices in a mesh: dp: 4 (over x, core), group: 8 (over z, y).
Axes of the slice: x: 2, y: 2, z: 4, core: 2. Of those that a mesh axis runs over, the one named last changes fastest.
Arguments:
- acts: bfloat16 [512, 2048], P('dp', 'group'), may hold values from -6 to 6
- cotan: bfloat16 [512, 2048], P('dp'), may hold values from -0.375 to 0.375
- stats: float32 [4, 8, 512, 512], P('dp', 'group'), as said below
- roots: bfloat16 [4, 8, 512, 512], P('dp', 'group'), as said below
- owner: int32 [8], replicated, may hold values from 0 to 7, as said below
- task_of: int32 [8], replicated, may hold values from 0 to 7, as said below
- counts: int32 [8], replicated, may hold values from 1 to 2
Outputs:
- update: bfloat16 [2048, 2048], P('dp', 'group')
- new_stats: float32 [4, 8, 512, 512], P('dp', 'group')
- new_roots: bfloat16 [4, 8, 512, 512], P('dp', 'group')
Inputs may be any that keep to these rules, and one draw needn't show every extreme that they name: A permutation; owner[t] is the group index of the device that keeps task t's statistic; task t is the left (t even) or right (t odd) factor of the block whose columns are held by group indices t - t % 2 and t - t % 2 + 1. `task_of`: the inverse permutation of owner. Each stats[k, o] is symmetric positive definite. Each roots[k, t] is symmetric.
All inputs are finite; a program needn't handle non-finite values.
Results may differ from a plain program's by a relative error of at most 0.0055.
The roundings to bfloat16 on the way count: a program that leaves them out, or rounds other values in their place, can miss the bound.
Values may be sent and summed in bfloat16 or wider, within the bound.
A program may use at most 128 MiB of HBM per device.

v0:
```python
import jax
import jax.numpy as jnp
from jax import lax
from jax.sharding import PartitionSpec as P

decay_rate = 0.9
ridge = 0.001
highest = lax.Precision.HIGHEST


def swapped(x, axis, distance):
    return lax.ppermute(x, axis, [(i, i ^ 1 << distance) for i in range(lax.axis_size(axis))])


def newton_root(statistic, turns):
    identity = jnp.eye(statistic.shape[0], dtype=jnp.float32)
    matrix = statistic + ridge * identity
    frobenius = jnp.sqrt(jnp.sum(matrix * matrix))
    scaled = matrix / frobenius
    step_matrix = (5.0 * identity - scaled) / 4.0
    root_now = step_matrix * frobenius ** (-0.25)

    def one_turn(index, current_state):
        root_now, scaled, step_matrix = current_state
        squared = jnp.dot(step_matrix, step_matrix, precision=highest)
        scaled = jnp.dot(squared, jnp.dot(squared, scaled, precision=highest), precision=highest)
        step_matrix = (5.0 * identity - scaled) / 4.0
        root_now = jnp.dot(root_now, step_matrix, precision=highest)
        return (root_now, scaled, step_matrix)

    return lax.fori_loop(1, turns, one_turn, (root_now, scaled, step_matrix))[0]


def route_blocks(payload, sources, groups):
    order_size, column_count = payload.shape
    strip_rows = order_size // groups
    spread_out = payload.reshape(groups, strip_rows, column_count)
    middle = lax.all_to_all(spread_out, "group", split_axis=0, concat_axis=0, tiled=True)
    chosen = middle[sources]
    arrived = lax.all_to_all(chosen, "group", split_axis=1, concat_axis=1, tiled=True)
    return arrived.reshape(sources.shape[0], order_size, column_count)


def per_device(acts, cotan, stats, roots, owner, task_of, counts):
    groups = lax.axis_size("group")
    position = lax.axis_index("group")
    order_size = stats.shape[-1]
    half_cols = acts.shape[1]
    column_half = position % 2
    row_block = lax.axis_index("dp")
    wanted = lax.dynamic_slice_in_dim(
        lax.all_gather(cotan, "dp", axis=0, tiled=True), row_block * order_size, order_size, 1
    )
    gradient = lax.dot_general(
        wanted,
        lax.all_gather(acts, "dp", axis=0, tiled=True),
        (((0,), (0,)), ((), ())),
        preferred_element_type=jnp.float32,
    ).astype(jnp.bfloat16)
    own_root = roots[0, 0]
    other_half, other_root = swapped((gradient, own_root), "group", 0)
    first_half = jnp.where(column_half == 0, gradient, other_half)
    second_half = jnp.where(column_half == 0, other_half, gradient)
    full_block = jnp.concatenate([first_half, second_half], 1)
    left_root = jnp.where(column_half == 0, own_root, other_root)
    right_root = jnp.where(column_half == 0, other_root, own_root)
    left_part = jnp.dot(left_root, full_block, preferred_element_type=jnp.float32).astype(
        jnp.bfloat16
    )
    right_columns = lax.dynamic_slice_in_dim(right_root, column_half * half_cols, half_cols, 1)
    update = jnp.dot(left_part, right_columns, preferred_element_type=jnp.float32).astype(
        jnp.bfloat16
    )
    my_task = task_of[position]
    factor_own = jnp.where(column_half == 1, full_block.T, full_block)
    factor = route_blocks(factor_own, task_of[None, :], groups)[0]
    gram_product = lax.dot_general(
        factor, factor, (((1,), (1,)), ((), ())), preferred_element_type=jnp.float32
    )
    refreshed_statistic = decay_rate * stats[0, 0] + gram_product
    fresh_root = newton_root(refreshed_statistic, counts[my_task]).astype(jnp.bfloat16)
    returned = route_blocks(fresh_root, owner[None, :], groups)[0]
    return (update, refreshed_statistic[None, None], returned[None, None])


def solution(mesh):
    return jax.shard_map(
        per_device,
        mesh=mesh,
        in_specs=(
            P("dp", "group"),
            P("dp", None),
            P("dp", "group", None, None),
            P("dp", "group", None, None),
            P(),
            P(),
            P(),
        ),
        out_specs=(P("dp", "group"), P("dp", "group", None, None), P("dp", "group", None, None)),
        check_vma=False,
    )
```

profile of v0, /device:TPU:1, one launch (start us, length us, event | category | flops | bytes accessed | tf_op | source)
XLA Modules:
  0.0 150.3 jit_solution(14024262070821917788)
XLA Ops:
  7.2 0.0 all-gather.2.cloned.1.call-start
  7.2 0.7 all-gather.2.cloned.1.call-update
  7.9 7.3 %all_gather.7 = bf16[512,256]{1,0:T(8,128)(2,1)S(1)} all-gather(bf16[128,256]{1,0:T(8,128)(2,1)} %param.9), channel_id=1, replica_groups=mesh['dp'=4,'group'=8] {'dp'}, dimensions={0}, use_global_device_ids=true | all-gather | bytes 327680 | tf_op jit(solution)/shard_map/all_gather | solution.py:56
  15.2 19.5 %all-gather.2.cloned.1.call-done = bf16[512,2048]{1,0:T(8,128)(2,1)} async-done(((bf16[128,2048]{1,0:T(8,128)(2,1)}), bf16[512,2048]{1,0:T(8,128)(2,1)}) %all-gather.2.cloned.1.call-update) | async-done | bytes 2097168 | tf_op jit(solution)/shard_map/all_gather | solution.py:52
  34.7 1.4 convolution_convert_fusion.1
  36.1 1.3 collective-permute-start.1
  37.3 6.4 %collective-permute-done.1 = bf16[512,256]{0,1:T(8,128)(2,1)S(1)} collective-permute-done((bf16[512,256]{0,1:T(8,128)(2,1)S(1)}, bf16[512,256]{0,1:T(8,128)(2,1)S(1)}, u32[]{:S(2)}, u32[]{:S(2)}) %collective-permute-start.1) | collective-permute-done | bytes 262176 | tf_op jit(solution)/shard_map/ppermute | solution.py:12
  43.8 0.0 copy-start
  43.8 0.2 copy.16
  44.1 0.0 copy-start.5
  44.1 0.1 bitcast_select_fusion
  44.2 0.0 copy-start.6
  44.2 1.0 copy.17
  45.2 0.0 copy-done
  45.2 0.0 copy-start.3
  45.2 5.4 %all-to-all-start = ((bf16[8,64,512]{2,1,0:T(8,128)(2,1)}), bf16[8,64,512]{2,1,0:T(8,128)(2,1)S(1)}, u32[]{:S(2)}, u32[]{:S(2)}) async-start(bf16[8,64,512]{2,1,0:T(8,128)(2,1)} %bitcast.3), calls=%async_computation | async-start | bytes 1048576 | tf_op jit(solution)/shard_map/all_to_all | solution.py:38
  50.6 0.0 copy-done.5
  50.6 13.3 %all-to-all-done = bf16[8,64,512]{2,1,0:T(8,128)(2,1)S(1)} async-done(((bf16[8,64,512]{2,1,0:T(8,128)(2,1)}), bf16[8,64,512]{2,1,0:T(8,128)(2,1)S(1)}, u32[]{:S(2)}, u32[]{:S(2)}) %all-to-all-start) | async-done | bytes 524320 | tf_op jit(solution)/shard_map/all_to_all | solution.py:38
  63.9 1.4 gather_fusion
  65.3 4.7 %all-to-all-start.1 = ((bf16[1,8,64,512]{3,2,0,1:T(8,128)(2,1)}), bf16[1,8,64,512]{3,2,0,1:T(8,128)(2,1)S(1)}, u32[]{:S(2)}, u32[]{:S(2)}) async-start(bf16[1,8,64,512]{3,2,0,1:T(8,128)(2,1)} %bitcast.5), calls=%async_computation.1 | async-start | bytes 1048576 | tf_op jit(solution)/shard_map/all_to_all | solution.py:40
  70.0 0.6 dynamic_slice.14
  72.5 0.0 copy-done.6
  72.5 0.6 dynamic_slice.15
  73.1 10.3 %all-to-all-done.1 = bf16[1,8,64,512]{3,2,0,1:T(8,128)(2,1)S(1)} async-done(((bf16[1,8,64,512]{3,2,0,1:T(8,128)(2,1)}), bf16[1,8,64,512]{3,2,0,1:T(8,128)(2,1)S(1)}, u32[]{:S(2)}, u32[]{:S(2)}) %all-to-all-start.1) | async-done | bytes 524320 | tf_op jit(solution)/shard_map/all_to_all | solution.py:40
  83.4 0.0 copy-done.3
  83.4 1.2 multiply_reduce_fusion
  84.6 0.0 copy-start.2
  85.3 0.3 fusion.5
  85.7 0.0 copy-done.2
  85.7 1.1 fusion.6
  86.8 1.6 %copy.19 = f32[512,512]{0,1:T(8,128)S(1)} copy(f32[512,512]{1,0:T(8,128)} %fusion.6) | data formatting | bytes 2097152
  88.4 0.6 while.15
  89.0 0.0 copy-start.7
  89.0 0.0 copy-start.4
  89.1 0.0 copy-start.1
  89.1 1.0 copy.20
  90.1 12.9 %all-to-all-start.2 = ((bf16[8,64,512]{2,1,0:T(8,128)(2,1)}), bf16[8,64,512]{2,1,0:T(8,128)(2,1)S(1)}, u32[]{:S(2)}, u32[]{:S(2)}) async-start(bf16[8,64,512]{2,1,0:T(8,128)(2,1)} %bitcast.10), calls=%async_computation.2 | async-start | bytes 1048576 | tf_op jit(solution)/shard_map/all_to_all | solution.py:38
  103.0 0.0 copy-done.7
  103.0 13.4 %all-to-all-done.2 = bf16[8,64,512]{2,1,0:T(8,128)(2,1)S(1)} async-done(((bf16[8,64,512]{2,1,0:T(8,128)(2,1)}), bf16[8,64,512]{2,1,0:T(8,128)(2,1)S(1)}, u32[]{:S(2)}, u32[]{:S(2)}) %all-to-all-start.2) | async-done | bytes 524320 | tf_op jit(solution)/shard_map/all_to_all | solution.py:38
  116.4 1.4 gather_fusion.1
  117.8 4.9 %all-to-all-start.3 = ((bf16[1,8,64,512]{3,2,0,1:T(8,128)(2,1)}), bf16[1,8,64,512]{3,2,0,1:T(8,128)(2,1)S(1)}, u32[]{:S(2)}, u32[]{:S(2)}) async-start(bf16[1,8,64,512]{3,2,0,1:T(8,128)(2,1)} %bitcast.12), calls=%async_computation.3 | async-start | bytes 1048576 | tf_op jit(solution)/shard_map/all_to_all | solution.py:40
  122.7 0.0 copy-done.4
  122.7 1.5 collective-permute-start
  124.2 17.0 %collective-permute-done = bf16[512,512]{1,0:T(8,128)(2,1)S(1)} collective-permute-done((bf16[512,512]{1,0:T(8,128)(2,1)S(1)}, bf16[512,512]{1,0:T(8,128)(2,1)S(1)}, u32[]{:S(2)}, u32[]{:S(2)}) %collective-permute-start) | collective-permute-done | bytes 524320 | tf_op jit(solution)/shard_map/ppermute | solution.py:12
  141.2 0.0 copy-done.1
  141.2 1.4 fusion.4
  142.6 0.0 all-to-all-done.3
  142.6 0.8 copy.37
  (6 shorter events, 0.1 us)
Async XLA Ops:
  7.2 27.5 %all-gather.2.cloned.1.call-start = ((), (), s32[]{:S(2)}) async-start(), calls=%async_computation.4 | async-start | bytes 2621440 | tf_op jit(solution)/shard_map/all_gather | solution.py:52
  36.1 7.7 %collective-permute-start.1 = (bf16[512,256]{0,1:T(8,128)(2,1)S(1)}, bf16[512,256]{0,1:T(8,128)(2,1)S(1)}, u32[]{:S(2)}, u32[]{:S(2)}) collective-permute-start(bf16[512,256]{0,1:T(8,128)(2,1)S(1)} %convolution_convert_fusion.1), channel_id=1, source_target_pairs={{0,1},{1,0},{2,3},{3,2},{4,5},{5,4},{6,7},{7,6},{8,9},{9,8},{10,11... | collective-permute-start | bytes 786440 | tf_op jit(solution)/shard_map/ppermute | solution.py:12
  43.8 1.4 copy-start
  44.1 6.5 %copy-start.5 = (s32[8]{0:T(128)S(1)}, s32[8]{0:T(128)}, u32[]{:S(2)}) copy-start(s32[8]{0:T(128)} %param.14) | copy-start | bytes 100
  44.2 28.3 %copy-start.6 = (s32[8]{0:T(128)S(1)}, s32[8]{0:T(128)}, u32[]{:S(2)}) copy-start(s32[8]{0:T(128)} %param.15) | copy-start | bytes 100
  45.2 38.2 %copy-start.3 = (f32[1,1,512,512]{3,2,1,0:T(8,128)S(1)}, f32[1,1,512,512]{3,2,1,0:T(8,128)}, u32[]{:S(2)}) copy-start(f32[1,1,512,512]{3,2,1,0:T(8,128)} %param.11) | copy-start | bytes 3145732
  45.2 18.7 %all-to-all-start = ((bf16[8,64,512]{2,1,0:T(8,128)(2,1)}), bf16[8,64,512]{2,1,0:T(8,128)(2,1)S(1)}, u32[]{:S(2)}, u32[]{:S(2)}) async-start(bf16[8,64,512]{2,1,0:T(8,128)(2,1)} %bitcast.3), calls=%async_computation | async-start | bytes 1048576 | tf_op jit(solution)/shard_map/all_to_all | solution.py:38
  65.3 18.1 %all-to-all-start.1 = ((bf16[1,8,64,512]{3,2,0,1:T(8,128)(2,1)}), bf16[1,8,64,512]{3,2,0,1:T(8,128)(2,1)S(1)}, u32[]{:S(2)}, u32[]{:S(2)}) async-start(bf16[1,8,64,512]{3,2,0,1:T(8,128)(2,1)} %bitcast.5), calls=%async_computation.1 | async-start | bytes 1048576 | tf_op jit(solution)/shard_map/all_to_all | solution.py:40
  84.6 1.1 copy-start.2
  89.0 14.0 %copy-start.7 = (s32[8]{0:T(128)S(1)}, s32[8]{0:T(128)}, u32[]{:S(2)}) copy-start(s32[8]{0:T(128)} %param.13) | copy-start | bytes 100
  89.0 33.7 %copy-start.4 = (bf16[1,1,512,512]{3,2,1,0:T(8,128)(2,1)S(1)}, bf16[1,1,512,512]{3,2,1,0:T(8,128)(2,1)}, u32[]{:S(2)}) copy-start(bf16[1,1,512,512]{3,2,1,0:T(8,128)(2,1)} %param.12) | copy-start | bytes 1572868
  89.1 52.1 %copy-start.1 = (bf16[512,256]{0,1:T(8,128)(2,1)S(1)}, bf16[512,256]{0,1:T(8,128)(2,1)}, u32[]{:S(2)}) copy-start(bf16[512,256]{0,1:T(8,128)(2,1)} %copy-done) | copy-start | bytes 786436
  90.1 26.4 %all-to-all-start.2 = ((bf16[8,64,512]{2,1,0:T(8,128)(2,1)}), bf16[8,64,512]{2,1,0:T(8,128)(2,1)S(1)}, u32[]{:S(2)}, u32[]{:S(2)}) async-start(bf16[8,64,512]{2,1,0:T(8,128)(2,1)} %bitcast.10), calls=%async_computation.2 | async-start | bytes 1048576 | tf_op jit(solution)/shard_map/all_to_all | solution.py:38
  117.8 24.8 %all-to-all-start.3 = ((bf16[1,8,64,512]{3,2,0,1:T(8,128)(2,1)}), bf16[1,8,64,512]{3,2,0,1:T(8,128)(2,1)S(1)}, u32[]{:S(2)}, u32[]{:S(2)}) async-start(bf16[1,8,64,512]{3,2,0,1:T(8,128)(2,1)} %bitcast.12), calls=%async_computation.3 | async-start | bytes 1048576 | tf_op jit(solution)/shard_map/all_to_all | solution.py:40
  122.7 18.5 %collective-permute-start = (bf16[512,512]{1,0:T(8,128)(2,1)S(1)}, bf16[512,512]{1,0:T(8,128)(2,1)S(1)}, u32[]{:S(2)}, u32[]{:S(2)}) collective-permute-start(bf16[512,512]{1,0:T(8,128)(2,1)S(1)} %bitcast.52), channel_id=1, source_target_pairs={{0,1},{1,0},{2,3},{3,2},{4,5},{5,4},{6,7},{7,6},{8,9},{9,8},{10,11... | collective-permute-start | bytes 1572872 | tf_op jit(solution)/shard_map/ppermute | solution.py:12
Sparse Core Ops, SparseCore 0:
  9.6 25.0 all-gather.1
where the time goes:
time: 151 us; the launch traced here: 150 us
  waiting for transfers between devices  80.6 us (53%)
  starting transfers between devices  30.6 us (20%)
  between operations  16.9 us (11%)
  local copies, waits for them, and re-layouts  8.54 us (6%)
  blocking collectives  7.3 us (5%)
  matrix products  4.04 us (3%)
  other arithmetic  1.67 us (1%)
    all_to_all x2, waiting for transfers between devices, route_blocks(): lax.all_to_all(spread_out, 'group', split_axis=0, concat_axis=0, tiled=True)  26.7 us
    ppermute x2, waiting for transfers between devices, swapped(): lax.ppermute(x, axis, [(i, i ^ 1 << distance) for i in range(lax.axis_siz...  23.5 us
    all_gather x1, waiting for transfers between devices, per_device(): lax.all_gather(cotan, 'dp', axis=0, tiled=True)  19.5 us
    all_to_all x2, starting transfers between devices, route_blocks(): lax.all_to_all(spread_out, 'group', split_axis=0, concat_axis=0, tiled=True)  18.3 us
    all_to_all x2, waiting for transfers between devices, route_blocks(): lax.all_to_all(chosen, 'group', split_axis=1, concat_axis=1, tiled=True)  10.3 us
    all_to_all x2, starting transfers between devices, route_blocks(): lax.all_to_all(chosen, 'group', split_axis=1, concat_axis=1, tiled=True)  9.55 us
    all_gather x1, blocking collectives, per_device(): lax.all_gather(acts, 'dp', axis=0, tiled=True)  7.3 us
  transfers between devices with their start and end apart: 7, of which 6 were waited for; matrix products, arithmetic and copies ran while one was open for 2% of the time, Pallas kernels for 0%

commit v1 on v0

--- a/solution.py
+++ b/solution.py
@@ -5,7 +5,6 @@
 
 decay_rate = 0.9
 ridge = 0.001
-highest = lax.Precision.HIGHEST
 
 
 def swapped(x, axis, distance):
@@ -18,17 +17,16 @@
     frobenius = jnp.sqrt(jnp.sum(matrix * matrix))
     scaled = matrix / frobenius
     step_matrix = (5.0 * identity - scaled) / 4.0
-    root_now = step_matrix * frobenius ** (-0.25)
-
-    def one_turn(index, current_state):
-        root_now, scaled, step_matrix = current_state
-        squared = jnp.dot(step_matrix, step_matrix, precision=highest)
-        scaled = jnp.dot(squared, jnp.dot(squared, scaled, precision=highest), precision=highest)
-        step_matrix = (5.0 * identity - scaled) / 4.0
-        root_now = jnp.dot(root_now, step_matrix, precision=highest)
-        return (root_now, scaled, step_matrix)
-
-    return lax.fori_loop(1, turns, one_turn, (root_now, scaled, step_matrix))[0]
+    low = scaled.astype(jnp.bfloat16)
+    square = jnp.dot(low, low, preferred_element_type=jnp.float32)
+    rest = ((square - 10.0 * scaled) / 16.0).astype(jnp.bfloat16)
+    product = (5.0 * scaled - square) / 4.0
+    for _ in range(2):
+        product = 1.5625 * product + jnp.dot(
+            rest, product.astype(jnp.bfloat16), preferred_element_type=jnp.float32
+        )
+    second = (5.0 * step_matrix - product) / 4.0
+    return jnp.where(turns == 1, step_matrix, second) * frobenius ** (-0.25)
 
 
 def route_blocks(payload, sources, groups):
@@ -36,7 +34,9 @@
     strip_rows = order_size // groups
     spread_out = payload.reshape(groups, strip_rows, column_count)
     middle = lax.all_to_all(spread_out, "group", split_axis=0, concat_axis=0, tiled=True)
-    chosen = middle[sources]
+    chosen = jnp.concatenate(
+        [lax.dynamic_slice_in_dim(middle, sources[0, each], 1, 0) for each in range(groups)], 0
+    )[None]
     arrived = lax.all_to_all(chosen, "group", split_axis=1, concat_axis=1, tiled=True)
     return arrived.reshape(sources.shape[0], order_size, column_count)
 
@@ -47,10 +47,7 @@
     order_size = stats.shape[-1]
     half_cols = acts.shape[1]
     column_half = position % 2
-    row_block = lax.axis_index("dp")
-    wanted = lax.dynamic_slice_in_dim(
-        lax.all_gather(cotan, "dp", axis=0, tiled=True), row_block * order_size, order_size, 1
-    )
+    wanted = lax.all_to_all(cotan, "dp", split_axis=1, concat_axis=0, tiled=True)
     gradient = lax.dot_general(
         wanted,
         lax.all_gather(acts, "dp", axis=0, tiled=True),

time: 151 us -> 136 us (0.901)
  the two profiles are of different devices: /device:TPU:1 before, /device:TPU:0 now
where the time goes in v1:
time: 136 us; the launch traced here: 135 us
  between operations  34.1 us (25%)
  waiting for transfers between devices  32.6 us (24%)
  starting transfers between devices  30.4 us (22%)
  local copies, waits for them, and re-layouts  18.3 us (13%)
  blocking collectives  11.1 us (8%)
  matrix products  8.13 us (6%)
    ppermute x2, waiting for transfers between devices, swapped(): lax.ppermute(x, axis, [(i, i ^ 1 << distance) for i in range(lax.axis_siz...  22.7 us
    unnamed x30, local copies, waits for them, and re-layouts  13 us
    all_to_all x2, starting transfers between devices, route_blocks(): lax.all_to_all(chosen, 'group', split_axis=1, concat_axis=1, tiled=True)  12.1 us
    all_gather x1, blocking collectives, per_device(): lax.all_gather(acts, 'dp', axis=0, tiled=True)  11.1 us
    all_to_all x2, waiting for transfers between devices, route_blocks(): lax.all_to_all(chosen, 'group', split_axis=1, concat_axis=1, tiled=True)  9.88 us
    all_to_all x2, starting transfers between devices, route_blocks(): lax.all_to_all(spread_out, 'group', split_axis=0, concat_axis=0, tiled=True)  9.67 us
    dot_general x2, matrix products, newton_root(): jnp.dot(rest, product.astype(jnp.bfloat16), preferred_element_type=jnp.fl...  4.7 us
    all_to_all x1, starting transfers between devices, per_device(): lax.all_to_all(cotan, 'dp', split_axis=1, concat_axis=0, tiled=True)  4.34 us
  transfers between devices with their start and end apart: 7, of which 3 were waited for; matrix products, arithmetic and copies ran while one was open for 3% of the time, Pallas kernels for 0%

profile of v1, /device:TPU:0, one launch (start us, length us, event | category | flops | bytes accessed | tf_op | source)
XLA Modules:
  0.0 134.8 jit_solution(7421427986286241481)
XLA Ops:
  0.6 2.0 %copy.17 = bf16[128,2048]{0,1:T(8,128)(2,1)} copy(bf16[128,2048]{1,0:T(8,128)(2,1)} %param.8) | data formatting | bytes 1048576 | tf_op args[1]
  2.7 0.0 copy-start
  2.7 4.3 %all-to-all-start = ((bf16[128,4,512]{0,2,1:T(8,128)(2,1)}), bf16[128,4,512]{0,2,1:T(8,128)(2,1)S(1)}, u32[]{:S(2)}, u32[]{:S(2)}) async-start(bf16[128,4,512]{0,2,1:T(8,128)(2,1)} %bitcast.1), calls=%async_computation | async-start | bytes 1048576 | tf_op jit(solution)/shard_map/all_to_all | solution.py:50
  7.0 0.0 copy-done
  7.0 11.1 %all_gather.3 = bf16[512,256]{1,0:T(8,128)(2,1)S(1)} all-gather(bf16[128,256]{1,0:T(8,128)(2,1)S(1)} %copy-done), channel_id=1, replica_groups=mesh['dp'=4,'group'=8] {'dp'}, dimensions={0}, use_global_device_ids=true | all-gather | bytes 327680 | tf_op jit(solution)/shard_map/all_gather | solution.py:53
  18.1 0.0 all-to-all-done
  18.1 0.2 copy.18
  18.3 0.3 convolution_convert_fusion.1
  18.7 2.3 %collective-permute-start.1 = (bf16[512,256]{0,1:T(8,128)(2,1)S(1)}, bf16[512,256]{0,1:T(8,128)(2,1)S(1)}, u32[]{:S(2)}, u32[]{:S(2)}) collective-permute-start(bf16[512,256]{0,1:T(8,128)(2,1)S(1)} %convolution_convert_fusion.1), channel_id=1, source_target_pairs={{0,1},{1,0},{2,3},{3,2},{4,5},{5,4},{6,7},{7,6},{8,9},{9,8},{10,11... | collective-permute-start | bytes 786440 | tf_op jit(solution)/shard_map/ppermute | solution.py:11
  20.9 6.8 %collective-permute-done.1 = bf16[512,256]{0,1:T(8,128)(2,1)S(1)} collective-permute-done((bf16[512,256]{0,1:T(8,128)(2,1)S(1)}, bf16[512,256]{0,1:T(8,128)(2,1)S(1)}, u32[]{:S(2)}, u32[]{:S(2)}) %collective-permute-start.1) | collective-permute-done | bytes 262176 | tf_op jit(solution)/shard_map/ppermute | solution.py:11
  27.9 0.2 copy.19
  28.1 0.1 bitcast_select_fusion
  28.2 1.0 copy.20
  29.2 6.1 %all-to-all-start.1 = ((bf16[8,64,512]{2,1,0:T(8,128)(2,1)}), bf16[8,64,512]{2,1,0:T(8,128)(2,1)S(1)}, u32[]{:S(2)}, u32[]{:S(2)}) async-start(bf16[8,64,512]{2,1,0:T(8,128)(2,1)} %bitcast.6), calls=%async_computation.1 | async-start | bytes 1048576 | tf_op jit(solution)/shard_map/all_to_all | solution.py:36
  35.3 0.0 copy-start.1
  35.3 0.7 copy-done.1
  35.9 0.7 fusion.32
  51.7 0.0 copy-start.3
  51.7 0.0 all-to-all-done.1
  51.7 0.6 dynamic-slice_dynamic-update-slice_fusion.15
  52.4 0.6 dynamic-slice_dynamic-update-slice_fusion.14
  53.0 0.6 dynamic-slice_dynamic-update-slice_fusion.13
  53.6 0.6 dynamic-slice_dynamic-update-slice_fusion.12
  54.3 0.6 dynamic-slice_dynamic-update-slice_fusion.11
  54.9 0.6 dynamic-slice_dynamic-update-slice_fusion.10
  55.5 0.6 dynamic-slice_dynamic-update-slice_fusion.9
  56.2 0.6 dynamic-slice_dynamic-update-slice_fusion.8
  56.8 6.0 %all-to-all-start.2 = ((bf16[1,8,64,512]{3,2,0,1:T(8,128)(2,1)}), bf16[1,8,64,512]{3,2,0,1:T(8,128)(2,1)S(1)}, u32[]{:S(2)}, u32[]{:S(2)}) async-start(bf16[1,8,64,512]{3,2,0,1:T(8,128)(2,1)} %bitcast.17), calls=%async_computation.2 | async-start | bytes 1048576 | tf_op jit(solution)/shard_map/all_to_all | solution.py:40
  62.8 0.6 dynamic_slice.66
  64.7 0.0 copy-start.5
  65.4 0.0 copy-done.5
  65.4 0.6 dynamic_slice.67
  66.6 9.9 %all-to-all-done.2 = bf16[1,8,64,512]{3,2,0,1:T(8,128)(2,1)S(1)} async-done(((bf16[1,8,64,512]{3,2,0,1:T(8,128)(2,1)}), bf16[1,8,64,512]{3,2,0,1:T(8,128)(2,1)S(1)}, u32[]{:S(2)}, u32[]{:S(2)}) %all-to-all-start.2) | async-done | bytes 524320 | tf_op jit(solution)/shard_map/all_to_all | solution.py:40
  76.5 0.0 copy-done.3
  76.5 1.2 multiply_reduce_fusion
  77.7 0.0 copy-start.6
  78.4 0.5 fusion.11
  78.9 1.6 %convolution_add_fusion.1 = f32[512,512]{1,0:T(8,128)} fusion(f32[512,512]{1,0:T(8,128)S(1)} %fusion.11, f32[]{:T(128)S(6)} %sqrt.3, f32[512,512]{1,0:T(8,128)S(1)} %get-tuple-element.22), kind=kOutput, calls=%fused_computation.3 | convolution fusion | flops 274726912 | bytes 3145732 | tf_op jit(solution)/shard_map/dot_general | solution.py:25
  80.5 0.0 copy-done.6
  80.6 3.1 %fusion.4 = bf16[512,512]{1,0:T(8,128)(2,1)} fusion(f32[512,512]{1,0:T(8,128)} %convolution_add_fusion.1, f32[]{:T(128)S(6)} %pow.3, f32[512,512]{1,0:T(8,128)S(1)} %fusion.11, pred[]{:T(512)} %bitcast.21, f32[]{:T(128)S(6)} %sqrt.3, f32[512,512]{1,0:T(8,128)S(1)} %get-tuple-element.22), kind=kOutput, calls=%fused_computation.7 | convolution fusion | flops 274726912 | bytes 3670025 | tf_op jit(solution)/shard_map/dot_general | solution.py:25
  83.6 3.6 %all-to-all-start.3 = ((bf16[8,64,512]{2,1,0:T(8,128)(2,1)}), bf16[8,64,512]{2,1,0:T(8,128)(2,1)S(1)}, u32[]{:S(2)}, u32[]{:S(2)}) async-start(bf16[8,64,512]{2,1,0:T(8,128)(2,1)} %bitcast.22), calls=%async_computation.3 | async-start | bytes 1048576 | tf_op jit(solution)/shard_map/all_to_all | solution.py:36
  87.2 0.0 copy-start.2
  87.2 0.7 copy-done.2
  87.9 0.7 fusion.31
  103.5 0.0 all-to-all-done.3
  103.5 0.6 dynamic-slice_dynamic-update-slice_fusion.7
  104.1 0.6 dynamic-slice_dynamic-update-slice_fusion.6
  104.8 0.6 dynamic-slice_dynamic-update-slice_fusion.5
  105.4 0.6 dynamic-slice_dynamic-update-slice_fusion.4
  106.0 0.6 dynamic-slice_dynamic-update-slice_fusion.3
  106.7 0.6 dynamic-slice_dynamic-update-slice_fusion.2
  107.3 0.6 dynamic-slice_dynamic-update-slice_fusion.1
  107.9 0.6 dynamic-slice_dynamic-update-slice_fusion
  108.6 0.0 copy-start.4
  108.6 6.1 %all-to-all-start.4 = ((bf16[1,8,64,512]{3,2,0,1:T(8,128)(2,1)}), bf16[1,8,64,512]{3,2,0,1:T(8,128)(2,1)S(1)}, u32[]{:S(2)}, u32[]{:S(2)}) async-start(bf16[1,8,64,512]{3,2,0,1:T(8,128)(2,1)} %bitcast.32), calls=%async_computation.4 | async-start | bytes 1048576 | tf_op jit(solution)/shard_map/all_to_all | solution.py:40
  114.7 0.0 copy-done.4
  114.7 2.0 %collective-permute-start = (bf16[512,512]{1,0:T(8,128)(2,1)S(1)}, bf16[512,512]{1,0:T(8,128)(2,1)S(1)}, u32[]{:S(2)}, u32[]{:S(2)}) collective-permute-start(bf16[512,512]{1,0:T(8,128)(2,1)S(1)} %bitcast.47), channel_id=1, source_target_pairs={{0,1},{1,0},{2,3},{3,2},{4,5},{5,4},{6,7},{7,6},{8,9},{9,8},{10,11... | collective-permute-start | bytes 1572872 | tf_op jit(solution)/shard_map/ppermute | solution.py:11
  116.7 15.9 %collective-permute-done = bf16[512,512]{1,0:T(8,128)(2,1)S(1)} collective-permute-done((bf16[512,512]{1,0:T(8,128)(2,1)S(1)}, bf16[512,512]{1,0:T(8,128)(2,1)S(1)}, u32[]{:S(2)}, u32[]{:S(2)}) %collective-permute-start) | collective-permute-done | bytes 524320 | tf_op jit(solution)/shard_map/ppermute | solution.py:11
  132.6 1.4 %fusion.6 = bf16[512,256]{1,0:T(8,128)(2,1)} fusion(bf16[512,512]{1,0:T(8,128)(2,1)S(1)} %bitcast.48, bf16[512,512]{1,0:T(8,128)(2,1)S(1)} %collective-permute-done, pred[]{:T(512)S(6)} %eq.22, s32[]{:T(128)S(6)} %select_n.109, bf16[512,256]{0,1:T(8,128)(2,1)S(1)} %get-tuple-element.4, bf16[512,256]{0,1:T(8,128)(2,1)S(1)} %get-tuple-element.3), kind=kOutput, calls=%fused_computation.10 | convolution fusion | flops 404488192 | bytes 2360832 | tf_op jit(solution)/shard_map/dot_general | solution.py:68
  134.0 0.0 all-to-all-done.4
  134.0 0.8 copy.37
  (2 shorter events, 0.1 us)
Async XLA Ops:
  2.7 4.3 %copy-start = (bf16[128,256]{1,0:T(8,128)(2,1)S(1)}, bf16[128,256]{1,0:T(8,128)(2,1)}, u32[]{:S(2)}) copy-start(bf16[128,256]{1,0:T(8,128)(2,1)} %param.7) | copy-start | bytes 196612
  2.7 15.4 %all-to-all-start = ((bf16[128,4,512]{0,2,1:T(8,128)(2,1)}), bf16[128,4,512]{0,2,1:T(8,128)(2,1)S(1)}, u32[]{:S(2)}, u32[]{:S(2)}) async-start(bf16[128,4,512]{0,2,1:T(8,128)(2,1)} %bitcast.1), calls=%async_computation | async-start | bytes 1048576 | tf_op jit(solution)/shard_map/all_to_all | solution.py:50
  18.7 9.1 %collective-permute-start.1 = (bf16[512,256]{0,1:T(8,128)(2,1)S(1)}, bf16[512,256]{0,1:T(8,128)(2,1)S(1)}, u32[]{:S(2)}, u32[]{:S(2)}) collective-permute-start(bf16[512,256]{0,1:T(8,128)(2,1)S(1)} %convolution_convert_fusion.1), channel_id=1, source_target_pairs={{0,1},{1,0},{2,3},{3,2},{4,5},{5,4},{6,7},{7,6},{8,9},{9,8},{10,11... | collective-permute-start | bytes 786440 | tf_op jit(solution)/shard_map/ppermute | solution.py:11
  29.2 22.5 %all-to-all-start.1 = ((bf16[8,64,512]{2,1,0:T(8,128)(2,1)}), bf16[8,64,512]{2,1,0:T(8,128)(2,1)S(1)}, u32[]{:S(2)}, u32[]{:S(2)}) async-start(bf16[8,64,512]{2,1,0:T(8,128)(2,1)} %bitcast.6), calls=%async_computation.1 | async-start | bytes 1048576 | tf_op jit(solution)/shard_map/all_to_all | solution.py:36
  35.3 0.7 copy-start.1
  51.7 24.8 %copy-start.3 = (f32[1,1,512,512]{3,2,1,0:T(8,128)S(1)}, f32[1,1,512,512]{3,2,1,0:T(8,128)}, u32[]{:S(2)}) copy-start(f32[1,1,512,512]{3,2,1,0:T(8,128)} %param.9) | copy-start | bytes 3145732
  56.8 19.7 %all-to-all-start.2 = ((bf16[1,8,64,512]{3,2,0,1:T(8,128)(2,1)}), bf16[1,8,64,512]{3,2,0,1:T(8,128)(2,1)S(1)}, u32[]{:S(2)}, u32[]{:S(2)}) async-start(bf16[1,8,64,512]{3,2,0,1:T(8,128)(2,1)} %bitcast.17), calls=%async_computation.2 | async-start | bytes 1048576 | tf_op jit(solution)/shard_map/all_to_all | solution.py:40
  64.7 0.7 copy-start.5
  77.7 2.8 %copy-start.6 = (f32[512,512]{1,0:T(8,128)}, f32[512,512]{1,0:T(8,128)S(1)}, u32[]{:S(2)}) copy-start(f32[512,512]{1,0:T(8,128)S(1)} %get-tuple-element.22) | copy-start | bytes 3145732
  83.6 19.9 %all-to-all-start.3 = ((bf16[8,64,512]{2,1,0:T(8,128)(2,1)}), bf16[8,64,512]{2,1,0:T(8,128)(2,1)S(1)}, u32[]{:S(2)}, u32[]{:S(2)}) async-start(bf16[8,64,512]{2,1,0:T(8,128)(2,1)} %bitcast.22), calls=%async_computation.3 | async-start | bytes 1048576 | tf_op jit(solution)/shard_map/all_to_all | solution.py:36
  87.2 0.7 copy-start.2
  108.6 6.1 %copy-start.4 = (bf16[1,1,512,512]{3,2,1,0:T(8,128)(2,1)S(1)}, bf16[1,1,512,512]{3,2,1,0:T(8,128)(2,1)}, u32[]{:S(2)}) copy-start(bf16[1,1,512,512]{3,2,1,0:T(8,128)(2,1)} %param.10) | copy-start | bytes 1572868
  108.6 25.5 %all-to-all-start.4 = ((bf16[1,8,64,512]{3,2,0,1:T(8,128)(2,1)}), bf16[1,8,64,512]{3,2,0,1:T(8,128)(2,1)S(1)}, u32[]{:S(2)}, u32[]{:S(2)}) async-start(bf16[1,8,64,512]{3,2,0,1:T(8,128)(2,1)} %bitcast.32), calls=%async_computation.4 | async-start | bytes 1048576 | tf_op jit(solution)/shard_map/all_to_all | solution.py:40
  114.7 17.9 %collective-permute-start = (bf16[512,512]{1,0:T(8,128)(2,1)S(1)}, bf16[512,512]{1,0:T(8,128)(2,1)S(1)}, u32[]{:S(2)}, u32[]{:S(2)}) collective-permute-start(bf16[512,512]{1,0:T(8,128)(2,1)S(1)} %bitcast.47), channel_id=1, source_target_pairs={{0,1},{1,0},{2,3},{3,2},{4,5},{5,4},{6,7},{7,6},{8,9},{9,8},{10,11... | collective-permute-start | bytes 1572872 | tf_op jit(solution)/shard_map/ppermute | solution.py:11

commit v2 on v1

v2 whole, which is shorter than its diff:
```python
import functools

import jax
import jax.numpy as jnp
from jax import lax
from jax.experimental import pallas as pl
from jax.experimental.pallas import tpu as pltpu
from jax.sharding import PartitionSpec as P

decay_rate = 0.9
ridge = 0.001
tile = 128
f32 = jnp.float32
bf16 = jnp.bfloat16


def dot(a, b, over=((1,), (0,))):
    return lax.dot_general(a, b, (over, ((), ())), preferred_element_type=f32)


def newton_root(matrix, turns, identity):
    size = jnp.sqrt(jnp.sum(matrix * matrix, keepdims=True))
    scaled = matrix * (1.0 / size)
    first = 1.25 * identity - 0.25 * scaled
    low = scaled.astype(bf16)
    square = dot(low, low)
    rest = ((square - 10.0 * scaled) * 0.0625).astype(bf16)
    product = 1.25 * scaled - 0.25 * square
    for _ in range(2):
        product = 1.5625 * product + dot(rest, product.astype(bf16))
    second = 1.25 * first - 0.25 * product
    return jnp.where(turns == 1, first, second) * (1.0 / jnp.sqrt(jnp.sqrt(size)))


def kernel(
    groups, dps, blocks,
    owner, task_of, counts, acts, cotan, stats, roots,
    update, new_stats, new_roots,
    acts_all, pairs, cot_all, lows, mid, staged, final, root_pair, block_ref,
    acts_send, acts_recv, pair_send, pair_recv, cot_send, cot_recv,
    one_send, one_recv, two_send, two_recv, root_send, root_recv,
):
    me = lax.axis_index("group")
    row = lax.axis_index("dp")
    order = stats.shape[-1]
    half = acts.shape[1]
    parity = lax.rem(me, 2)
    partner = me + 1 - 2 * parity
    first = me - parity

    def group_at(d):
        return lax.rem(me + d, groups)

    def row_at(d):
        return lax.rem(row + d, dps)

    def copy(src, dst, send, recv, axis, to):
        return pltpu.make_async_remote_copy(
            src_ref=src, dst_ref=dst, send_sem=send, recv_sem=recv,
            device_id={axis: to}, device_id_type=pl.DeviceIdType.MESH,
        )

    barrier = pltpu.get_barrier_semaphore()
    for d in range(1, groups):
        pl.semaphore_signal(barrier, inc=1, device_id={"group": group_at(d)}, device_id_type=pl.DeviceIdType.MESH)
    for d in range(1, dps):
        pl.semaphore_signal(barrier, inc=1, device_id={"dp": row_at(d)}, device_id_type=pl.DeviceIdType.MESH)
    for at, (i, j) in enumerate(blocks):
        part = stats[i * tile : (i + 1) * tile, j * tile : (j + 1) * tile].astype(bf16)
        lows[at * tile : (at + 1) * tile, :] = part
    strip = lows.shape[0] // groups
    pl.semaphore_wait(barrier, groups + dps - 2)

    def strip_of(g):
        return lows.at[pl.ds(pl.multiple_of(g * strip, strip), strip), :]

    act_copies = [
        copy(acts, acts_all.at[me], acts_send.at[d], acts_recv.at[d], "group", group_at(d))
        for d in range(1, groups)
    ]
    cot_copies = []
    for d in range(1, dps):
        to = row_at(d)
        columns = cotan.at[:, pl.ds(pl.multiple_of(to * order, order), order)]
        cot_copies.append(copy(columns, cot_all.at[row], cot_send.at[d], cot_recv.at[d], "dp", to))
    one_copies = [
        copy(strip_of(group_at(d)), mid.at[me], one_send.at[d], one_recv.at[d], "group", group_at(d))
        for d in range(1, groups)
    ]
    root_copy = copy(roots, root_pair.at[parity], root_send.at[0], root_recv.at[0], "group", partner)
    for each in [*act_copies, *one_copies, *cot_copies, root_copy]:
        each.start()

    acts_all[me] = acts[...]
    mid[me] = lows[pl.ds(pl.multiple_of(me * strip, strip), strip), :]
    root_pair[parity] = roots[...]
    cot_all[row] = cotan[:, pl.ds(pl.multiple_of(row * order, order), order)]
    mine = task_of[me]
    task_first = mine - lax.rem(mine, 2)

    def arrived(buffer, back, send, recv, axis, d):
        copy(buffer.at[back], buffer.at[back], send.at[d], recv.at[d], axis, back).wait_recv()

    for d in range(1, groups):
        arrived(acts_all, lax.rem(me + groups - d, groups), acts_send, acts_recv, "group", d)
    for i in range(2):
        pairs[row, i] = acts_all[first + i]
        pairs[row, 2 + i] = acts_all[task_first + i]
    pair_copies = [
        copy(pairs.at[row], pairs.at[row], pair_send.at[d], pair_recv.at[d], "dp", row_at(d))
        for d in range(1, dps)
    ]
    for each in pair_copies:
        each.start()
    for d in range(1, groups):
        arrived(mid, lax.rem(me + groups - d, groups), one_send, one_recv, "group", d)
    two_copies = []
    for d in range(1, groups):
        staged[d] = mid[owner[group_at(d)]]
        each = copy(staged.at[d], final.at[me], two_send.at[d], two_recv.at[d], "group", group_at(d))
        each.start()
        two_copies.append(each)
    final[me] = mid[owner[me]]

    for d in range(1, dps):
        arrived(cot_all, lax.rem(row + dps - d, dps), cot_send, cot_recv, "dp", d)
    tokens = dps * acts.shape[0]
    cot_t = cot_all[...].reshape(tokens, order).T
    for d in range(1, dps):
        arrived(pairs, lax.rem(row + dps - d, dps), pair_send, pair_recv, "dp", d)

    def gradient_into(start):
        for i in range(2):
            part = dot(cot_t, pairs[:, start + i].reshape(tokens, half))
            block_ref[:, i * half : (i + 1) * half] = part.astype(bf16)
        return block_ref[...]

    def gram(block, side):
        return jnp.where(side == 1, dot(block, block, ((0,), (0,))), dot(block, block, ((1,), (1,))))

    new_stats[...] = decay_rate * stats[...] + gram(gradient_into(2), lax.rem(mine, 2))
    own = gradient_into(0)
    own_gram = gram(own, parity)
    copy(roots, root_pair.at[1 - parity], root_send.at[0], root_recv.at[0], "group", partner).wait_recv()
    left_part = dot(root_pair[0], own).astype(bf16)
    right = root_pair[1, :, pl.ds(pl.multiple_of(parity * half, half), half)]
    update[...] = dot(left_part, right).astype(bf16)

    for d in range(1, groups):
        arrived(final, lax.rem(me + groups - d, groups), two_send, two_recv, "group", d)
    packed = final[...].reshape(lows.shape).astype(f32)
    found = {b: packed[at * tile : (at + 1) * tile] for at, b in enumerate(blocks)}
    count = range(order // tile)
    whole = jnp.concatenate(
        [
            jnp.concatenate([found[i, j] if (i, j) in found else found[j, i].T for j in count], 1)
            for i in count
        ],
        0,
    )
    shape = (order, order)
    eye = lax.broadcasted_iota(jnp.int32, shape, 0) == lax.broadcasted_iota(jnp.int32, shape, 1)
    identity = jnp.where(eye, 1.0, 0.0).astype(f32)
    matrix = decay_rate * whole + own_gram + ridge * identity
    new_roots[...] = newton_root(matrix, counts[me], identity).astype(bf16)
    for each in [*act_copies, *one_copies, *cot_copies, root_copy, *pair_copies, *two_copies]:
        each.wait_send()


def per_device(acts, cotan, stats, roots, owner, task_of, counts):
    groups, dps = lax.axis_size("group"), lax.axis_size("dp")
    order, half = stats.shape[-1], acts.shape[1]
    count = range(order // tile)
    blocks = [(i, j) for i in count for j in count if j >= i]
    if len(blocks) * tile % (16 * groups):
        blocks = [(i, j) for i in count for j in count]
    rows = len(blocks) * tile
    strips = pltpu.VMEM((groups, rows // groups, tile), bf16)
    in_vmem, in_smem = (pl.BlockSpec(memory_space=m) for m in (pltpu.VMEM, pltpu.SMEM))
    over_group, over_dp = (pltpu.SemaphoreType.DMA((n,)) for n in (groups, dps))
    update, new_stats, new_roots = pl.pallas_call(
        functools.partial(kernel, groups, dps, blocks),
        out_shape=(
            jax.ShapeDtypeStruct((order, half), bf16),
            jax.ShapeDtypeStruct((order, order), f32),
            jax.ShapeDtypeStruct((order, order), bf16),
        ),
        in_specs=[in_smem] * 3 + [in_vmem] * 4,
        out_specs=(in_vmem,) * 3,
        scratch_shapes=[
            pltpu.VMEM((groups, *acts.shape), bf16),
            pltpu.VMEM((dps, 4, *acts.shape), bf16),
            pltpu.VMEM((dps, acts.shape[0], order), bf16),
            pltpu.VMEM((rows, tile), bf16),
            strips,
            strips,
            strips,
            pltpu.VMEM((2, order, order), bf16),
            pltpu.VMEM((order, order), bf16),
            *[over_group] * 2,
            *[over_dp] * 4,
            *[over_group] * 4,
            *[pltpu.SemaphoreType.DMA((1,))] * 2,
        ],
        compiler_params=pltpu.CompilerParams(
            collective_id=0, has_side_effects=True, vmem_limit_bytes=48 * 2**20
        ),
    )(owner, task_of, counts, acts, cotan, stats[0, 0], roots[0, 0])
    return update, new_stats[None, None], new_roots[None, None]


def solution(mesh):
    return jax.shard_map(
        per_device,
        mesh=mesh,
        in_specs=(
            P("dp", "group"),
            P("dp", None),
            P("dp", "group", None, None),
            P("dp", "group", None, None),
            P(),
            P(),
            P(),
        ),
        out_specs=(P("dp", "group"), P("dp", "group", None, None), P("dp", "group", None, None)),
        check_vma=False,
    )
```

time: 136 us -> 47 us (0.35)
  the two profiles are of different devices: /device:TPU:0 before, /device:TPU:13 now
where the time goes in v2:
time: 47 us; the launch traced here: 46.7 us
  Pallas kernels  38.8 us (83%)
  local copies, waits for them, and re-layouts  7.28 us (15%)
  between operations  0.67 us (1%)
    pallas_call x1, Pallas kernels, per_device(): pl.pallas_call(functools.partial(kernel, groups, dps, blocks), out_shape=...  38.8 us
    unnamed x17, local copies, waits for them, and re-layouts  7.28 us

profile of v2, /device:TPU:13, one launch (start us, length us, event | category | flops | bytes accessed | tf_op | source)
XLA Modules:
  0.0 46.7 jit_solution(11738822552870647567)
XLA Ops:
  0.6 0.0 copy-start.4
  0.6 0.0 copy-start.5
  0.7 0.0 copy-start.6
  0.7 0.6 %copy-done.4 = s32[8]{0:T(128)S(1)} copy-done((s32[8]{0:T(128)S(1)}, s32[8]{0:T(128)}, u32[]{:S(2)}) %copy-start.4) | copy-done | bytes 56
  1.3 0.0 copy-done.5
  1.3 0.0 copy-done.6
  1.3 0.0 copy-start
  1.3 1.2 %copy-done = f32[1,1,512,512]{3,2,1,0:T(8,128)S(1)} copy-done((f32[1,1,512,512]{3,2,1,0:T(8,128)S(1)}, f32[1,1,512,512]{3,2,1,0:T(8,128)}, u32[]{:S(2)}) %copy-start) | copy-done | bytes 1048600
  2.5 0.0 copy-start.1
  2.5 1.0 %copy-done.1 = bf16[128,2048]{1,0:T(8,128)(2,1)S(1)} copy-done((bf16[128,2048]{1,0:T(8,128)(2,1)S(1)}, bf16[128,2048]{1,0:T(8,128)(2,1)}, u32[]{:S(2)}) %copy-start.1) | copy-done | bytes 524312
  3.6 0.0 copy-start.2
  3.6 1.0 %copy-done.2 = bf16[1,1,512,512]{3,2,1,0:T(8,128)(2,1)S(1)} copy-done((bf16[1,1,512,512]{3,2,1,0:T(8,128)(2,1)S(1)}, bf16[1,1,512,512]{3,2,1,0:T(8,128)(2,1)}, u32[]{:S(2)}) %copy-start.2) | copy-done | bytes 524312
  4.6 0.0 copy-start.3
  4.6 0.8 %copy-done.3 = bf16[128,256]{1,0:T(8,128)(2,1)S(1)} copy-done((bf16[128,256]{1,0:T(8,128)(2,1)S(1)}, bf16[128,256]{1,0:T(8,128)(2,1)}, u32[]{:S(2)}) %copy-start.3) | copy-done | bytes 65560
  5.5 38.8 %shard_map.94 = (bf16[512,256]{1,0:T(8,128)(2,1)S(1)}, f32[512,512]{1,0:T(8,128)S(1)}, bf16[512,512]{1,0:T(8,128)(2,1)S(1)}) custom-call(s32[8]{0:T(128)S(1)} %copy-done.4, s32[8]{0:T(128)S(1)} %copy-done.5, s32[8]{0:T(128)S(1)} %copy-done.6, bf16[128,256]{1,0:T(8,128)(2,1)S(1)} %copy-done.3, bf16[128,2048]{1,0:T(8,128)(2,1)S(1)} %copy-done.1, ...), custom_call_target="tpu_custom_call" | custom-call | tf_op jit(solution)/shard_map/pallas_call | solution.py:181
  44.3 0.7 %copy.13 = bf16[512,256]{1,0:T(8,128)(2,1)} copy(bf16[512,256]{1,0:T(8,128)(2,1)S(1)} %get-tuple-element.12) | data formatting | bytes 524288
  45.0 1.0 %copy.14 = f32[1,1,512,512]{3,2,1,0:T(8,128)} copy(f32[1,1,512,512]{3,2,1,0:T(8,128)S(1)} %bitcast.5) | data formatting | bytes 2097152
  45.9 0.8 %copy.15 = bf16[1,1,512,512]{3,2,1,0:T(8,128)(2,1)} copy(bf16[1,1,512,512]{3,2,1,0:T(8,128)(2,1)S(1)} %bitcast.7) | data formatting | bytes 1048576
Async XLA Ops:
  0.6 0.7 %copy-start.4 = (s32[8]{0:T(128)S(1)}, s32[8]{0:T(128)}, u32[]{:S(2)}) copy-start(s32[8]{0:T(128)} %owner.1) | copy-start | bytes 100
  0.6 0.7 %copy-start.5 = (s32[8]{0:T(128)S(1)}, s32[8]{0:T(128)}, u32[]{:S(2)}) copy-start(s32[8]{0:T(128)} %task_of.1) | copy-start | bytes 100
  0.7 0.7 %copy-start.6 = (s32[8]{0:T(128)S(1)}, s32[8]{0:T(128)}, u32[]{:S(2)}) copy-start(s32[8]{0:T(128)} %counts.1) | copy-start | bytes 100
  1.3 1.2 %copy-start = (f32[1,1,512,512]{3,2,1,0:T(8,128)S(1)}, f32[1,1,512,512]{3,2,1,0:T(8,128)}, u32[]{:S(2)}) copy-start(f32[1,1,512,512]{3,2,1,0:T(8,128)} %param.9) | copy-start | bytes 3145732
  2.5 1.0 %copy-start.1 = (bf16[128,2048]{1,0:T(8,128)(2,1)S(1)}, bf16[128,2048]{1,0:T(8,128)(2,1)}, u32[]{:S(2)}) copy-start(bf16[128,2048]{1,0:T(8,128)(2,1)} %cotan.1) | copy-start | bytes 1572868
  3.6 1.0 %copy-start.2 = (bf16[1,1,512,512]{3,2,1,0:T(8,128)(2,1)S(1)}, bf16[1,1,512,512]{3,2,1,0:T(8,128)(2,1)}, u32[]{:S(2)}) copy-start(bf16[1,1,512,512]{3,2,1,0:T(8,128)(2,1)} %param.10) | copy-start | bytes 1572868
  4.6 0.8 %copy-start.3 = (bf16[128,256]{1,0:T(8,128)(2,1)S(1)}, bf16[128,256]{1,0:T(8,128)(2,1)}, u32[]{:S(2)}) copy-start(bf16[128,256]{1,0:T(8,128)(2,1)} %acts.1) | copy-start | bytes 196612

commit v3 on v2

--- a/solution.py
+++ b/solution.py
@@ -36,9 +36,10 @@
     groups, dps, blocks,
     owner, task_of, counts, acts, cotan, stats, roots,
     update, new_stats, new_roots,
-    acts_all, pairs, cot_all, lows, mid, staged, final, root_pair, block_ref,
-    acts_send, acts_recv, pair_send, pair_recv, cot_send, cot_recv,
-    one_send, one_recv, two_send, two_recv, root_send, root_recv,
+    act_mid, act_staged, act_final, pairs, cot_all, lows, mid, staged, final, root_low, root_in, root_pair, block_ref,
+    acts_send, acts_recv, pick_send, pick_recv, one_send, one_recv, two_send, two_recv,
+    own_send, own_recv, other_send, other_recv, task_send, task_recv, cot_send, cot_recv,
+    near_send, near_recv, root_send, root_recv,
 ):
     me = lax.axis_index("group")
     row = lax.axis_index("dp")
@@ -68,15 +69,27 @@
     for at, (i, j) in enumerate(blocks):
         part = stats[i * tile : (i + 1) * tile, j * tile : (j + 1) * tile].astype(bf16)
         lows[at * tile : (at + 1) * tile, :] = part
+        root_low[at * tile : (at + 1) * tile, :] = roots[i * tile : (i + 1) * tile, j * tile : (j + 1) * tile]
     strip = lows.shape[0] // groups
     pl.semaphore_wait(barrier, groups + dps - 2)
 
     def strip_of(g):
         return lows.at[pl.ds(pl.multiple_of(g * strip, strip), strip), :]
 
+    cut = act_final.shape[1]
+    depth = act_final.shape[3]
+
+    def act_strip(g):
+        return pl.ds(pl.multiple_of(g * depth, depth), depth) if cut > 1 else slice(None)
+
     act_copies = [
-        copy(acts, acts_all.at[me], acts_send.at[d], acts_recv.at[d], "group", group_at(d))
+        copy(acts.at[act_strip(group_at(d)), :], act_mid.at[me], acts_send.at[d], acts_recv.at[d], "group", group_at(d))
         for d in range(1, groups)
+    ]
+    near_copy = copy(acts, pairs.at[row, parity], near_send.at[0], near_recv.at[0], "group", partner)
+    own_copies = [
+        copy(acts, pairs.at[row, parity], own_send.at[d], own_recv.at[d], "dp", row_at(d))
+        for d in range(1, dps)
     ]
     cot_copies = []
     for d in range(1, dps):
@@ -87,33 +100,62 @@
         copy(strip_of(group_at(d)), mid.at[me], one_send.at[d], one_recv.at[d], "group", group_at(d))
         for d in range(1, groups)
     ]
-    root_copy = copy(roots, root_pair.at[parity], root_send.at[0], root_recv.at[0], "group", partner)
-    for each in [*act_copies, *one_copies, *cot_copies, root_copy]:
-        each.start()
-
-    acts_all[me] = acts[...]
+    root_copy = copy(root_low, root_in, root_send.at[0], root_recv.at[0], "group", partner)
+    for each in [near_copy, *act_copies, *one_copies, *cot_copies, *own_copies, root_copy]:
+        each.start()
+
+    pairs[row, parity] = acts[...]
+    act_mid[me] = acts[act_strip(me), :]
     mid[me] = lows[pl.ds(pl.multiple_of(me * strip, strip), strip), :]
     root_pair[parity] = roots[...]
     cot_all[row] = cotan[:, pl.ds(pl.multiple_of(row * order, order), order)]
     mine = task_of[me]
-    task_first = mine - lax.rem(mine, 2)
-
-    def arrived(buffer, back, send, recv, axis, d):
-        copy(buffer.at[back], buffer.at[back], send.at[d], recv.at[d], axis, back).wait_recv()
-
-    for d in range(1, groups):
-        arrived(acts_all, lax.rem(me + groups - d, groups), acts_send, acts_recv, "group", d)
-    for i in range(2):
-        pairs[row, i] = acts_all[first + i]
-        pairs[row, 2 + i] = acts_all[task_first + i]
-    pair_copies = [
-        copy(pairs.at[row], pairs.at[row], pair_send.at[d], pair_recv.at[d], "dp", row_at(d))
+
+    def back(d):
+        return lax.rem(me + groups - d, groups)
+
+    def row_back(d):
+        return lax.rem(row + dps - d, dps)
+
+    def arrived(place, send, recv, axis, source):
+        copy(place, place, send, recv, axis, source).wait_recv()
+
+    other = pairs.at[row, 1 - parity]
+    arrived(other, near_send.at[0], near_recv.at[0], "group", partner)
+    other_copies = [
+        copy(other, other, other_send.at[d], other_recv.at[d], "dp", row_at(d)) for d in range(1, dps)
+    ]
+    for each in other_copies:
+        each.start()
+
+    for d in range(1, groups):
+        arrived(act_mid.at[back(d)], acts_send.at[d], acts_recv.at[d], "group", back(d))
+    start = mine - lax.rem(mine, 2)
+    pick_copies = []
+    if cut > 1:
+        for d in range(1, groups):
+            task = task_of[group_at(d)]
+            base = task - lax.rem(task, 2)
+            for i in range(2):
+                act_staged[d, i] = act_mid[base + i]
+            each = copy(act_staged.at[d], act_final.at[row, me], pick_send.at[d], pick_recv.at[d], "group", group_at(d))
+            each.start()
+            pick_copies.append(each)
+        for i in range(2):
+            act_final[row, me, i] = act_mid[start + i]
+        for d in range(1, groups):
+            arrived(act_final.at[row, back(d)], pick_send.at[d], pick_recv.at[d], "group", back(d))
+    else:
+        for i in range(2):
+            act_final[row, 0, i] = act_mid[start + i]
+    task_copies = [
+        copy(act_final.at[row], act_final.at[row], task_send.at[d], task_recv.at[d], "dp", row_at(d))
         for d in range(1, dps)
     ]
-    for each in pair_copies:
-        each.start()
-    for d in range(1, groups):
-        arrived(mid, lax.rem(me + groups - d, groups), one_send, one_recv, "group", d)
+    for each in task_copies:
+        each.start()
+    for d in range(1, groups):
+        arrived(mid.at[back(d)], one_send.at[d], one_recv.at[d], "group", back(d))
     two_copies = []
     for d in range(1, groups):
         staged[d] = mid[owner[group_at(d)]]
@@ -123,47 +165,51 @@
     final[me] = mid[owner[me]]
 
     for d in range(1, dps):
-        arrived(cot_all, lax.rem(row + dps - d, dps), cot_send, cot_recv, "dp", d)
+        arrived(cot_all.at[row_back(d)], cot_send.at[d], cot_recv.at[d], "dp", row_back(d))
     tokens = dps * acts.shape[0]
     cot_t = cot_all[...].reshape(tokens, order).T
     for d in range(1, dps):
-        arrived(pairs, lax.rem(row + dps - d, dps), pair_send, pair_recv, "dp", d)
-
-    def gradient_into(start):
+        arrived(pairs.at[row_back(d), parity], own_send.at[d], own_recv.at[d], "dp", row_back(d))
+        arrived(pairs.at[row_back(d), 1 - parity], other_send.at[d], other_recv.at[d], "dp", row_back(d))
+
+    def gradient_of(halves):
         for i in range(2):
-            part = dot(cot_t, pairs[:, start + i].reshape(tokens, half))
+            part = dot(cot_t, halves[i].reshape(tokens, half))
             block_ref[:, i * half : (i + 1) * half] = part.astype(bf16)
         return block_ref[...]
 
     def gram(block, side):
         return jnp.where(side == 1, dot(block, block, ((0,), (0,))), dot(block, block, ((1,), (1,))))
 
-    new_stats[...] = decay_rate * stats[...] + gram(gradient_into(2), lax.rem(mine, 2))
-    own = gradient_into(0)
+    def unpacked(packed):
+        found = {b: packed[at * tile : (at + 1) * tile] for at, b in enumerate(blocks)}
+        count = range(order // tile)
+        rows = [[found[i, j] if (i, j) in found else found[j, i].T for j in count] for i in count]
+        return jnp.concatenate([jnp.concatenate(each, 1) for each in rows], 0)
+
+    own = gradient_of([pairs[:, i] for i in range(2)])
     own_gram = gram(own, parity)
-    copy(roots, root_pair.at[1 - parity], root_send.at[0], root_recv.at[0], "group", partner).wait_recv()
+    arrived(root_in, root_send.at[0], root_recv.at[0], "group", partner)
+    root_pair[1 - parity] = unpacked(root_in[...].astype(f32)).astype(bf16)
     left_part = dot(root_pair[0], own).astype(bf16)
     right = root_pair[1, :, pl.ds(pl.multiple_of(parity * half, half), half)]
     update[...] = dot(left_part, right).astype(bf16)
 
-    for d in range(1, groups):
-        arrived(final, lax.rem(me + groups - d, groups), two_send, two_recv, "group", d)
-    packed = final[...].reshape(lows.shape).astype(f32)
-    found = {b: packed[at * tile : (at + 1) * tile] for at, b in enumerate(blocks)}
-    count = range(order // tile)
-    whole = jnp.concatenate(
-        [
-            jnp.concatenate([found[i, j] if (i, j) in found else found[j, i].T for j in count], 1)
-            for i in count
-        ],
-        0,
-    )
+    for d in range(1, dps):
+        arrived(act_final.at[row_back(d)], task_send.at[d], task_recv.at[d], "dp", row_back(d))
+    task_block = gradient_of([act_final[:, :, i] for i in range(2)])
+    new_stats[...] = decay_rate * stats[...] + gram(task_block, lax.rem(mine, 2))
+
+    for d in range(1, groups):
+        arrived(final.at[back(d)], two_send.at[d], two_recv.at[d], "group", back(d))
+    whole = unpacked(final[...].reshape(lows.shape).astype(f32))
     shape = (order, order)
     eye = lax.broadcasted_iota(jnp.int32, shape, 0) == lax.broadcasted_iota(jnp.int32, shape, 1)
     identity = jnp.where(eye, 1.0, 0.0).astype(f32)
     matrix = decay_rate * whole + own_gram + ridge * identity
     new_roots[...] = newton_root(matrix, counts[me], identity).astype(bf16)
-    for each in [*act_copies, *one_copies, *cot_copies, root_copy, *pair_copies, *two_copies]:
+    sent = [near_copy, root_copy, *act_copies, *own_copies, *other_copies, *pick_copies]
+    for each in [*sent, *task_copies, *cot_copies, *one_copies, *two_copies]:
         each.wait_send()
 
 
@@ -175,6 +221,8 @@
     if len(blocks) * tile % (16 * groups):
         blocks = [(i, j) for i in count for j in count]
     rows = len(blocks) * tile
+    cut = groups if acts.shape[0] % (16 * groups) == 0 else 1
+    depth = acts.shape[0] // cut
     strips = pltpu.VMEM((groups, rows // groups, tile), bf16)
     in_vmem, in_smem = (pl.BlockSpec(memory_space=m) for m in (pltpu.VMEM, pltpu.SMEM))
     over_group, over_dp = (pltpu.SemaphoreType.DMA((n,)) for n in (groups, dps))
@@ -188,19 +236,22 @@
         in_specs=[in_smem] * 3 + [in_vmem] * 4,
         out_specs=(in_vmem,) * 3,
         scratch_shapes=[
-            pltpu.VMEM((groups, *acts.shape), bf16),
-            pltpu.VMEM((dps, 4, *acts.shape), bf16),
+            pltpu.VMEM((groups, depth, half), bf16),
+            pltpu.VMEM((cut, 2, depth, half), bf16),
+            pltpu.VMEM((dps, cut, 2, depth, half), bf16),
+            pltpu.VMEM((dps, 2, *acts.shape), bf16),
             pltpu.VMEM((dps, acts.shape[0], order), bf16),
             pltpu.VMEM((rows, tile), bf16),
             strips,
             strips,
             strips,
+            pltpu.VMEM((rows, tile), bf16),
+            pltpu.VMEM((rows, tile), bf16),
             pltpu.VMEM((2, order, order), bf16),
             pltpu.VMEM((order, order), bf16),
-            *[over_group] * 2,
-            *[over_dp] * 4,
-            *[over_group] * 4,
-            *[pltpu.SemaphoreType.DMA((1,))] * 2,
+            *[over_group] * 8,
+            *[over_dp] * 8,
+            *[pltpu.SemaphoreType.DMA((1,))] * 4,
         ],
         compiler_params=pltpu.CompilerParams(
             collective_id=0, has_side_effects=True, vmem_limit_bytes=48 * 2**20

time: 47 us -> 40.9 us (0.87)
  the two profiles are of different devices: /device:TPU:13 before, /device:TPU:1 now
where the time goes in v3:
time: 40.9 us; the launch traced here: 40.6 us
  Pallas kernels  32.7 us (80%)
  local copies, waits for them, and re-layouts  7.28 us (18%)
  between operations  0.67 us (2%)
    pallas_call x1, Pallas kernels, per_device(): pl.pallas_call(functools.partial(kernel, groups, dps, blocks), out_shape=...  32.7 us
    unnamed x17, local copies, waits for them, and re-layouts  7.28 us

profile of v3, /device:TPU:1, one launch (start us, length us, event | category | flops | bytes accessed | tf_op | source)
XLA Modules:
  0.0 40.6 jit_solution(16832920401193746847)
XLA Ops:
  0.6 0.0 copy-start.4
  0.6 0.0 copy-start.5
  0.7 0.0 copy-start.6
  0.7 0.6 %copy-done.4 = s32[8]{0:T(128)S(1)} copy-done((s32[8]{0:T(128)S(1)}, s32[8]{0:T(128)}, u32[]{:S(2)}) %copy-start.4) | copy-done | bytes 56
  1.3 0.0 copy-done.5
  1.3 0.0 copy-done.6
  1.3 0.0 copy-start
  1.3 1.2 %copy-done = f32[1,1,512,512]{3,2,1,0:T(8,128)S(1)} copy-done((f32[1,1,512,512]{3,2,1,0:T(8,128)S(1)}, f32[1,1,512,512]{3,2,1,0:T(8,128)}, u32[]{:S(2)}) %copy-start) | copy-done | bytes 1048600
  2.5 0.0 copy-start.1
  2.5 1.0 %copy-done.1 = bf16[128,2048]{1,0:T(8,128)(2,1)S(1)} copy-done((bf16[128,2048]{1,0:T(8,128)(2,1)S(1)}, bf16[128,2048]{1,0:T(8,128)(2,1)}, u32[]{:S(2)}) %copy-start.1) | copy-done | bytes 524312
  3.6 0.0 copy-start.2
  3.6 1.0 %copy-done.2 = bf16[1,1,512,512]{3,2,1,0:T(8,128)(2,1)S(1)} copy-done((bf16[1,1,512,512]{3,2,1,0:T(8,128)(2,1)S(1)}, bf16[1,1,512,512]{3,2,1,0:T(8,128)(2,1)}, u32[]{:S(2)}) %copy-start.2) | copy-done | bytes 524312
  4.6 0.0 copy-start.3
  4.6 0.8 %copy-done.3 = bf16[128,256]{1,0:T(8,128)(2,1)S(1)} copy-done((bf16[128,256]{1,0:T(8,128)(2,1)S(1)}, bf16[128,256]{1,0:T(8,128)(2,1)}, u32[]{:S(2)}) %copy-start.3) | copy-done | bytes 65560
  5.5 32.7 %shard_map.94 = (bf16[512,256]{1,0:T(8,128)(2,1)S(1)}, f32[512,512]{1,0:T(8,128)S(1)}, bf16[512,512]{1,0:T(8,128)(2,1)S(1)}) custom-call(s32[8]{0:T(128)S(1)} %copy-done.4, s32[8]{0:T(128)S(1)} %copy-done.5, s32[8]{0:T(128)S(1)} %copy-done.6, bf16[128,256]{1,0:T(8,128)(2,1)S(1)} %copy-done.3, bf16[128,2048]{1,0:T(8,128)(2,1)S(1)} %copy-done.1, ...), custom_call_target="tpu_custom_call" | custom-call | tf_op jit(solution)/shard_map/pallas_call | solution.py:229
  38.1 0.7 %copy.13 = bf16[512,256]{1,0:T(8,128)(2,1)} copy(bf16[512,256]{1,0:T(8,128)(2,1)S(1)} %get-tuple-element.12) | data formatting | bytes 524288
  38.8 1.0 %copy.14 = f32[1,1,512,512]{3,2,1,0:T(8,128)} copy(f32[1,1,512,512]{3,2,1,0:T(8,128)S(1)} %bitcast.5) | data formatting | bytes 2097152
  39.8 0.8 %copy.15 = bf16[1,1,512,512]{3,2,1,0:T(8,128)(2,1)} copy(bf16[1,1,512,512]{3,2,1,0:T(8,128)(2,1)S(1)} %bitcast.7) | data formatting | bytes 1048576
Async XLA Ops:
  0.6 0.7 %copy-start.4 = (s32[8]{0:T(128)S(1)}, s32[8]{0:T(128)}, u32[]{:S(2)}) copy-start(s32[8]{0:T(128)} %owner.1) | copy-start | bytes 100
  0.6 0.7 %copy-start.5 = (s32[8]{0:T(128)S(1)}, s32[8]{0:T(128)}, u32[]{:S(2)}) copy-start(s32[8]{0:T(128)} %task_of.1) | copy-start | bytes 100
  0.7 0.7 %copy-start.6 = (s32[8]{0:T(128)S(1)}, s32[8]{0:T(128)}, u32[]{:S(2)}) copy-start(s32[8]{0:T(128)} %counts.1) | copy-start | bytes 100
  1.3 1.2 %copy-start = (f32[1,1,512,512]{3,2,1,0:T(8,128)S(1)}, f32[1,1,512,512]{3,2,1,0:T(8,128)}, u32[]{:S(2)}) copy-start(f32[1,1,512,512]{3,2,1,0:T(8,128)} %param.9) | copy-start | bytes 3145732
  2.5 1.0 %copy-start.1 = (bf16[128,2048]{1,0:T(8,128)(2,1)S(1)}, bf16[128,2048]{1,0:T(8,128)(2,1)}, u32[]{:S(2)}) copy-start(bf16[128,2048]{1,0:T(8,128)(2,1)} %cotan.1) | copy-start | bytes 1572868
  3.6 1.0 %copy-start.2 = (bf16[1,1,512,512]{3,2,1,0:T(8,128)(2,1)S(1)}, bf16[1,1,512,512]{3,2,1,0:T(8,128)(2,1)}, u32[]{:S(2)}) copy-start(bf16[1,1,512,512]{3,2,1,0:T(8,128)(2,1)} %param.10) | copy-start | bytes 1572868
  4.6 0.8 %copy-start.3 = (bf16[128,256]{1,0:T(8,128)(2,1)S(1)}, bf16[128,256]{1,0:T(8,128)(2,1)}, u32[]{:S(2)}) copy-start(bf16[128,256]{1,0:T(8,128)(2,1)} %acts.1) | copy-start | bytes 196612

commit v4 on v3

--- a/solution.py
+++ b/solution.py
@@ -34,12 +34,12 @@
 
 def kernel(
     groups, dps, blocks,
-    owner, task_of, counts, acts, cotan, stats, roots,
+    owner, task_of, counts, acts, cotan, stats_in, roots,
     update, new_stats, new_roots,
-    act_mid, act_staged, act_final, pairs, cot_all, lows, mid, staged, final, root_low, root_in, root_pair, block_ref,
+    act_mid, act_staged, act_final, pairs, cot_all, lows, mid, staged, final, root_low, root_in, root_pair, block_ref, stats,
     acts_send, acts_recv, pick_send, pick_recv, one_send, one_recv, two_send, two_recv,
     own_send, own_recv, other_send, other_recv, task_send, task_recv, cot_send, cot_recv,
-    near_send, near_recv, root_send, root_recv,
+    near_send, near_recv, root_send, root_recv, load_sem,
 ):
     me = lax.axis_index("group")
     row = lax.axis_index("dp")
@@ -66,10 +66,20 @@
         pl.semaphore_signal(barrier, inc=1, device_id={"group": group_at(d)}, device_id_type=pl.DeviceIdType.MESH)
     for d in range(1, dps):
         pl.semaphore_signal(barrier, inc=1, device_id={"dp": row_at(d)}, device_id_type=pl.DeviceIdType.MESH)
-    for at, (i, j) in enumerate(blocks):
-        part = stats[i * tile : (i + 1) * tile, j * tile : (j + 1) * tile].astype(bf16)
-        lows[at * tile : (at + 1) * tile, :] = part
-        root_low[at * tile : (at + 1) * tile, :] = roots[i * tile : (i + 1) * tile, j * tile : (j + 1) * tile]
+    columns = cotan.at[:, pl.ds(pl.multiple_of(row * order, order), order)]
+    stats_load, roots_load, acts_load, cotan_load = loads = [
+        pltpu.make_async_copy(src, dst, load_sem.at[i])
+        for i, (src, dst) in enumerate(
+            [
+                (stats_in, stats),
+                (roots, root_pair.at[parity]),
+                (acts, pairs.at[row, parity]),
+                (columns, cot_all.at[row]),
+            ]
+        )
+    ]
+    for each in loads:
+        each.start()
     strip = lows.shape[0] // groups
     pl.semaphore_wait(barrier, groups + dps - 2)
 
@@ -101,14 +111,23 @@
         for d in range(1, groups)
     ]
     root_copy = copy(root_low, root_in, root_send.at[0], root_recv.at[0], "group", partner)
-    for each in [near_copy, *act_copies, *one_copies, *cot_copies, *own_copies, root_copy]:
-        each.start()
-
-    pairs[row, parity] = acts[...]
-    act_mid[me] = acts[act_strip(me), :]
+    for each in [near_copy, *act_copies, *cot_copies, *own_copies]:
+        each.start()
+    stats_load.wait()
+    for at, (i, j) in enumerate(blocks):
+        part = stats[i * tile : (i + 1) * tile, j * tile : (j + 1) * tile].astype(bf16)
+        lows[at * tile : (at + 1) * tile, :] = part
+    for each in one_copies:
+        each.start()
     mid[me] = lows[pl.ds(pl.multiple_of(me * strip, strip), strip), :]
-    root_pair[parity] = roots[...]
-    cot_all[row] = cotan[:, pl.ds(pl.multiple_of(row * order, order), order)]
+    roots_load.wait()
+    for at, (i, j) in enumerate(blocks):
+        part = root_pair[parity, i * tile : (i + 1) * tile, j * tile : (j + 1) * tile]
+        root_low[at * tile : (at + 1) * tile, :] = part
+    root_copy.start()
+    acts_load.wait()
+    act_mid[me] = pairs[row, parity, act_strip(me), :]
+    cotan_load.wait()
     mine = task_of[me]
 
     def back(d):
@@ -233,7 +252,7 @@
             jax.ShapeDtypeStruct((order, order), f32),
             jax.ShapeDtypeStruct((order, order), bf16),
         ),
-        in_specs=[in_smem] * 3 + [in_vmem] * 4,
+        in_specs=[in_smem] * 3 + [pl.BlockSpec(memory_space=pltpu.HBM)] * 4,
         out_specs=(in_vmem,) * 3,
         scratch_shapes=[
             pltpu.VMEM((groups, depth, half), bf16),
@@ -249,12 +268,14 @@
             pltpu.VMEM((rows, tile), bf16),
             pltpu.VMEM((2, order, order), bf16),
             pltpu.VMEM((order, order), bf16),
+            pltpu.VMEM((order, order), f32),
             *[over_group] * 8,
             *[over_dp] * 8,
             *[pltpu.SemaphoreType.DMA((1,))] * 4,
+            pltpu.SemaphoreType.DMA((4,)),
         ],
         compiler_params=pltpu.CompilerParams(
-            collective_id=0, has_side_effects=True, vmem_limit_bytes=48 * 2**20
+            collective_id=0, has_side_effects=True, vmem_limit_bytes=54 * 2**20
         ),
     )(owner, task_of, counts, acts, cotan, stats[0, 0], roots[0, 0])
     return update, new_stats[None, None], new_roots[None, None]

time: 40.9 us -> 39.8 us (0.973)
  local copies, waits for them, and re-layouts: 7.28 us -> 4.79 us
  Pallas kernels: 32.7 us -> 34.2 us
    unnamed x17 -> x5, local copies, waits for them, and re-layouts: 7.28 us -> 4.79 us
    pallas_call x1, Pallas kernels: 32.7 us -> 34.2 us  [per_device(): pl.pallas_call(functools.partial(kernel, groups, dps, blocks), out_shape=...]
where the time goes in v4:
time: 39.8 us; the launch traced here: 39.7 us
  Pallas kernels  34.2 us (86%)
  local copies, waits for them, and re-layouts  4.79 us (12%)
  between operations  0.64 us (2%)
    pallas_call x1, Pallas kernels, per_device(): pl.pallas_call(functools.partial(kernel, groups, dps, blocks), out_shape=...  34.2 us
    unnamed x5, local copies, waits for them, and re-layouts  4.79 us

profile of v4, /device:TPU:1, one launch (start us, length us, event | category | flops | bytes accessed | tf_op | source)
XLA Modules:
  0.0 39.7 jit_solution(3813736047711435596)
XLA Ops:
  0.6 34.2 %shard_map.94 = (bf16[512,256]{1,0:T(8,128)(2,1)}, f32[512,512]{1,0:T(8,128)}, bf16[512,512]{1,0:T(8,128)(2,1)}) custom-call(s32[8]{0:T(128)} %owner.1, s32[8]{0:T(128)} %task_of.1, s32[8]{0:T(128)} %counts.1, bf16[128,256]{1,0:T(8,128)(2,1)} %acts.1, bf16[128,2048]{1,0:T(8,128)(2,1)} %cotan.1, f32[512,512]{1,0:T(8,128)} %bitcast.4, bf16[512,512]{1,0:T(8,128)(2,1)} %bitcast.6), custom_call_target="tpu_custom_call" | custom-call | tf_op jit(solution)/shard_map/pallas_call | solution.py:248
  34.9 1.7 %copy.13 = bf16[512,256]{1,0:T(8,128)(2,1)} copy(bf16[512,256]{1,0:T(8,128)(2,1)} %get-tuple-element.12) | data formatting | bytes 524288
  36.5 0.0 copy-start
  36.5 2.3 %copy.14 = f32[1,1,512,512]{3,2,1,0:T(8,128)} copy(f32[1,1,512,512]{3,2,1,0:T(8,128)} %bitcast.5) | data formatting | bytes 2097152
  38.9 0.0 copy-done
  38.9 0.8 %copy.15 = bf16[1,1,512,512]{3,2,1,0:T(8,128)(2,1)} copy(bf16[1,1,512,512]{3,2,1,0:T(8,128)(2,1)S(1)} %bitcast.7) | data formatting | bytes 1048576
Async XLA Ops:
  36.5 2.3 %copy-start = (bf16[512,512]{1,0:T(8,128)(2,1)S(1)}, bf16[512,512]{1,0:T(8,128)(2,1)}, u32[]{:S(2)}) copy-start(bf16[512,512]{1,0:T(8,128)(2,1)} %get-tuple-element.8) | copy-start | bytes 1572868

commit v5 on v4

--- a/solution.py
+++ b/solution.py
@@ -36,7 +36,7 @@
     groups, dps, blocks,
     owner, task_of, counts, acts, cotan, stats_in, roots,
     update, new_stats, new_roots,
-    act_mid, act_staged, act_final, pairs, cot_all, lows, mid, staged, final, root_low, root_in, root_pair, block_ref, stats,
+    act_mid, act_staged, act_final, pairs, cot_all, lows, mid, staged, final, root_low, root_in, root_pair, block_ref, stats, cot_turned,
     acts_send, acts_recv, pick_send, pick_recv, one_send, one_recv, two_send, two_recv,
     own_send, own_recv, other_send, other_recv, task_send, task_recv, cot_send, cot_recv,
     near_send, near_recv, root_send, root_recv, load_sem,
@@ -173,6 +173,10 @@
     ]
     for each in task_copies:
         each.start()
+    for d in range(1, dps):
+        arrived(cot_all.at[row_back(d)], cot_send.at[d], cot_recv.at[d], "dp", row_back(d))
+    tokens = dps * acts.shape[0]
+    cot_turned[...] = cot_all[...].reshape(tokens, order).T
     for d in range(1, groups):
         arrived(mid.at[back(d)], one_send.at[d], one_recv.at[d], "group", back(d))
     two_copies = []
@@ -184,16 +188,12 @@
     final[me] = mid[owner[me]]
 
     for d in range(1, dps):
-        arrived(cot_all.at[row_back(d)], cot_send.at[d], cot_recv.at[d], "dp", row_back(d))
-    tokens = dps * acts.shape[0]
-    cot_t = cot_all[...].reshape(tokens, order).T
-    for d in range(1, dps):
         arrived(pairs.at[row_back(d), parity], own_send.at[d], own_recv.at[d], "dp", row_back(d))
         arrived(pairs.at[row_back(d), 1 - parity], other_send.at[d], other_recv.at[d], "dp", row_back(d))
 
     def gradient_of(halves):
         for i in range(2):
-            part = dot(cot_t, halves[i].reshape(tokens, half))
+            part = dot(cot_turned[...], halves[i].reshape(tokens, half))
             block_ref[:, i * half : (i + 1) * half] = part.astype(bf16)
         return block_ref[...]
 
@@ -269,6 +269,7 @@
             pltpu.VMEM((2, order, order), bf16),
             pltpu.VMEM((order, order), bf16),
             pltpu.VMEM((order, order), f32),
+            pltpu.VMEM((order, dps * acts.shape[0]), bf16),
             *[over_group] * 8,
             *[over_dp] * 8,
             *[pltpu.SemaphoreType.DMA((1,))] * 4,

time: 39.8 us -> 39.8 us (level)
  no operation moved by 1% of the time
where the time goes in v5:
time: 39.8 us; the launch traced here: 39.7 us
  Pallas kernels  34.2 us (86%)
  local copies, waits for them, and re-layouts  4.79 us (12%)
  between operations  0.64 us (2%)
    pallas_call x1, Pallas kernels, per_device(): pl.pallas_call(functools.partial(kernel, groups, dps, blocks), out_shape=...  34.2 us
    unnamed x5, local copies, waits for them, and re-layouts  4.79 us

profile of v5, /device:TPU:1, one launch (start us, length us, event | category | flops | bytes accessed | tf_op | source)
XLA Modules:
  0.0 39.7 jit_solution(3308802276167362187)
XLA Ops:
  0.6 34.2 %shard_map.94 = (bf16[512,256]{1,0:T(8,128)(2,1)}, f32[512,512]{1,0:T(8,128)}, bf16[512,512]{1,0:T(8,128)(2,1)}) custom-call(s32[8]{0:T(128)} %owner.1, s32[8]{0:T(128)} %task_of.1, s32[8]{0:T(128)} %counts.1, bf16[128,256]{1,0:T(8,128)(2,1)} %acts.1, bf16[128,2048]{1,0:T(8,128)(2,1)} %cotan.1, f32[512,512]{1,0:T(8,128)} %bitcast.4, bf16[512,512]{1,0:T(8,128)(2,1)} %bitcast.6), custom_call_target="tpu_custom_call" | custom-call | tf_op jit(solution)/shard_map/pallas_call | solution.py:248
  34.9 1.7 %copy.13 = bf16[512,256]{1,0:T(8,128)(2,1)} copy(bf16[512,256]{1,0:T(8,128)(2,1)} %get-tuple-element.12) | data formatting | bytes 524288
  36.5 0.0 copy-start
  36.5 2.3 %copy.14 = f32[1,1,512,512]{3,2,1,0:T(8,128)} copy(f32[1,1,512,512]{3,2,1,0:T(8,128)} %bitcast.5) | data formatting | bytes 2097152
  38.9 0.0 copy-done
  38.9 0.8 %copy.15 = bf16[1,1,512,512]{3,2,1,0:T(8,128)(2,1)} copy(bf16[1,1,512,512]{3,2,1,0:T(8,128)(2,1)S(1)} %bitcast.7) | data formatting | bytes 1048576
Async XLA Ops:
  36.5 2.3 %copy-start = (bf16[512,512]{1,0:T(8,128)(2,1)S(1)}, bf16[512,512]{1,0:T(8,128)(2,1)}, u32[]{:S(2)}) copy-start(bf16[512,512]{1,0:T(8,128)(2,1)} %get-tuple-element.8) | copy-start | bytes 1572868
